TPU v7x, 32 devices: a whole 2x2x4 slice. The times are simulated.
32 devices in a mesh: replica: 8 (over z, core), fsdp: 4 (over y, x).
Axes of the slice: x: 2, y: 2, z: 4, core: 2. Of those that a mesh axis runs over, the one named last changes fastest.
Arguments:
- tokens: bfloat16 [4096, 8192], P(('replica', 'fsdp')), may hold values from -6 to 6
- target: bfloat16 [4096, 512], P(('replica', 'fsdp')), may hold values from -6 to 6
- weight: bfloat16 [8, 8192, 512], P('replica', 'fsdp'), may hold values from -6 to 6
- pseudo: float32 [8, 8192, 512], P('replica', 'fsdp'), may hold values from -6 to 6
- global_frag: float32 [8192, 512], P('fsdp'), may hold values from -6 to 6
- momentum: float32 [8192, 512], P('fsdp'), may hold values from -2 to 2
Outputs:
- new_weight: bfloat16 [8, 8192, 512], P('replica', 'fsdp')
- residual: bfloat16 [4096, 512], P(('replica', 'fsdp'))
- new_global: float32 [8192, 512], P('fsdp')
- new_momentum: float32 [8192, 512], P('fsdp')
All inputs are finite; a program needn't handle non-finite values.
Results may differ from a plain program's by a relative error of at most 0.013.
Values may be sent and summed in bfloat16 or wider, within the bound.
A program may use at most 128 MiB of HBM per device.

v0:
```python
import jax
import jax.numpy as jnp
from jax import lax
from jax.sharding import PartitionSpec as P

inner_rate = 1.0
outer_rate = 0.7
nesterov_coef = 0.9
merge_share = 0.5


def shards(tokens, target, weight, pseudo, global_frag, momentum):
    model_width = tokens.shape[1]
    key_scale = model_width ** (-0.5)
    weight_rows = weight[0]
    columns = lax.all_to_all(tokens, "fsdp", split_axis=1, concat_axis=0, tiled=True)
    keys_own = lax.psum_scatter(
        (jnp.dot(columns, weight_rows, preferred_element_type=jnp.float32) * key_scale).astype(
            jnp.bfloat16
        ),
        "fsdp",
        scatter_dimension=0,
        tiled=True,
    ).astype(jnp.float32)
    residual_own = (keys_own - target.astype(jnp.float32)).astype(jnp.bfloat16)
    residual_all = lax.all_gather(residual_own, "fsdp", axis=0, tiled=True)
    gradient = (
        lax.dot_general(
            columns, residual_all, (((0,), (0,)), ((), ())), preferred_element_type=jnp.float32
        )
        * key_scale
    )
    stepped = weight_rows.astype(jnp.float32) - inner_rate * gradient
    summed = lax.psum(pseudo[0], "replica")
    averaged = summed / lax.axis_size("replica")
    new_momentum = nesterov_coef * momentum + averaged
    new_global = global_frag - outer_rate * (averaged + nesterov_coef * new_momentum)
    new_weight = (merge_share * stepped + (1.0 - merge_share) * new_global).astype(jnp.bfloat16)
    return (new_weight[None], residual_own, new_global, new_momentum)


def solution(mesh):
    in_specs = (
        P(("replica", "fsdp"), None),
        P(("replica", "fsdp"), None),
        P("replica", "fsdp", None),
        P("replica", "fsdp", None),
        P("fsdp", None),
        P("fsdp", None),
    )
    out_specs = (
        P("replica", "fsdp", None),
        P(("replica", "fsdp"), None),
        P("fsdp", None),
        P("fsdp", None),
    )
    return jax.shard_map(shards, mesh=mesh, in_specs=in_specs, out_specs=out_specs, check_vma=False)
```

profile of v0, /device:TPU:0, one launch (start us, length us, event | category | flops | bytes accessed | tf_op | source)
XLA Modules:
  0.0 162.2 jit_solution(17577499728462123444)
XLA Ops:
  8.0 0.0 all-reduce.2.cloned.1.call-start
  8.0 5.3 %copy.27 = f32[1,2048,512]{1,2,0:T(8,128)} copy(f32[1,2048,512]{2,1,0:T(8,128)} %param.9) | data formatting | bytes 8388608 | tf_op args[3]
  13.4 0.0 copy-start.1
  13.4 0.0 all-reduce.2.cloned.1.call-update
  13.4 0.0 reduce-scatter.2.cloned.1.call-start
  13.5 1.5 copy-done.1
  15.0 2.4 %copy.25 = bf16[128,8192]{0,1:T(8,128)(2,1)} copy(bf16[128,8192]{1,0:T(8,128)(2,1)S(1)} %copy-done.1) | data formatting | bytes 4194304 | tf_op args[0]
  17.4 30.5 %all_to_all.19 = bf16[128,4,2048]{0,2,1:T(8,128)(2,1)S(1)} all-to-all(bf16[128,4,2048]{0,2,1:T(8,128)(2,1)} %bitcast.30), channel_id=1, replica_groups=mesh['replica'=8,'fsdp'=4] {'fsdp'}, dimensions={1} | all-to-all | bytes 4194304 | tf_op jit(solution)/shard_map/all_to_all | solution.py:16
  47.9 2.6 %copy.26 = bf16[4,128,2048]{2,1,0:T(8,128)(2,1)} copy(bf16[4,128,2048]{1,2,0:T(8,128)(2,1)S(1)} %bitcast.29) | data formatting | bytes 4194304 | tf_op jit(solution)/shard_map/all_to_all | solution.py:16
  50.5 0.0 copy-start.2
  50.5 4.5 %fusion.9 = bf16[512,512]{1,0:T(8,128)(2,1)} fusion(bf16[512,2048]{1,0:T(8,128)(2,1)} %bitcast.31, bf16[1,2048,512]{2,1,0:T(8,128)(2,1)} %param.8), kind=kOutput, calls=%fused_computation.10 | convolution fusion | flops 1074266112 | bytes 4718592 | tf_op jit(solution)/shard_map/dot_general | solution.py:18
  55.0 0.0 reduce-scatter.2.cloned.1.call-update
  55.0 0.0 copy-done.2
  55.0 2.5 %copy.24 = bf16[1,2048,512]{1,2,0:T(8,128)(2,1)} copy(bf16[1,2048,512]{2,1,0:T(8,128)(2,1)S(1)} %copy-done.2) | data formatting | bytes 4194304 | tf_op args[2]
  57.5 5.4 %copy.28 = f32[2048,512]{0,1:T(8,128)} copy(f32[2048,512]{1,0:T(8,128)} %param.11) | data formatting | bytes 8388608 | tf_op args[5]
  62.9 5.5 %copy.29 = f32[2048,512]{0,1:T(8,128)} copy(f32[2048,512]{1,0:T(8,128)} %param.10) | data formatting | bytes 8388608 | tf_op args[4]
  68.3 44.5 %all-reduce.2.cloned.1.call-done = f32[2048,512]{0,1:T(8,128)} async-done(((f32[2048,512]{0,1:T(8,128)}), f32[2048,512]{0,1:T(8,128)}) %all-reduce.2.cloned.1.call-update) | async-done | bytes 4194320 | tf_op jit(solution)/shard_map/psum | solution.py:34
  112.8 10.4 %multiply_add_fusion = (f32[2048,512]{0,1:T(8,128)}, f32[2048,512]{0,1:T(8,128)}) fusion(f32[2048,512]{0,1:T(8,128)} %copy.28, f32[2048,512]{0,1:T(8,128)} %all-reduce.2.cloned.1.call-done, f32[2048,512]{0,1:T(8,128)} %copy.29), kind=kLoop, calls=%fused_computation.5 | loop fusion | flops 7340032 | bytes 20971520 | tf_op jit(solution)/shard_map/add | solution.py:36
  123.2 5.3 %copy.31 = f32[2048,512]{1,0:T(8,128)} copy(f32[2048,512]{0,1:T(8,128)} %get-tuple-element.17) | data formatting | bytes 8388608
  128.5 0.0 copy-start.4
  128.5 0.0 copy-start
  128.5 5.5 %copy.32 = f32[2048,512]{1,0:T(8,128)} copy(f32[2048,512]{0,1:T(8,128)} %get-tuple-element.16) | data formatting | bytes 8388608
  134.0 0.0 reduce-scatter.2.cloned.1.call-done
  134.0 0.0 copy-done.4
  134.0 0.9 subtract_convert_fusion
  134.9 0.0 copy-start.3
  134.9 10.0 %all_gather.3 = bf16[512,512]{1,0:T(8,128)(2,1)S(1)} all-gather(bf16[128,512]{1,0:T(8,128)(2,1)S(1)} %subtract_convert_fusion), channel_id=1, replica_groups=mesh['replica'=8,'fsdp'=4] {'fsdp'}, dimensions={0}, use_global_device_ids=true | all-gather | bytes 655360 | tf_op jit(solution)/shard_map/all_gather | solution.py:26
  145.0 0.0 copy-done
  145.0 5.9 %fusion.3 = bf16[1,2048,512]{1,2,0:T(8,128)(2,1)} fusion(f32[2048,512]{0,1:T(8,128)} %get-tuple-element.17, bf16[512,512]{1,0:T(8,128)(2,1)S(1)} %all_gather.3, bf16[512,2048]{1,0:T(8,128)(2,1)S(1)} %bitcast.32, bf16[1,2048,512]{1,2,0:T(8,128)(2,1)} %copy.24), kind=kOutput, calls=%fused_computation.6 | convolution fusion | flops 1080033280 | bytes 11010048 | tf_op jit(solution)/shard_map/dot_general | solution.py:28
  150.8 0.0 copy-done.3
  150.8 3.9 %copy.30 = bf16[1,2048,512]{2,1,0:T(8,128)(2,1)} copy(bf16[1,2048,512]{1,2,0:T(8,128)(2,1)} %fusion.3) | data formatting | bytes 4194304
Async XLA Ops:
  8.0 104.8 %all-reduce.2.cloned.1.call-start = ((), (), s32[]{:S(2)}) async-start(), calls=%async_computation.3 | async-start | bytes 8388608 | tf_op jit(solution)/shard_map/psum | solution.py:34
  13.4 1.6 copy-start.1
  13.4 120.6 %reduce-scatter.2.cloned.1.call-start = ((), (), s32[]{:S(2)}) async-start(), calls=%async_computation.2 | async-start | bytes 655360 | tf_op jit(solution)/shard_map/reduce_scatter | solution.py:17
  50.5 4.5 %copy-start.2 = (bf16[1,2048,512]{2,1,0:T(8,128)(2,1)S(1)}, bf16[1,2048,512]{2,1,0:T(8,128)(2,1)}, u32[]{:S(2)}) copy-start(bf16[1,2048,512]{2,1,0:T(8,128)(2,1)} %param.8) | copy-start | bytes 6291460
  128.5 5.5 %copy-start.4 = (bf16[128,512]{1,0:T(8,128)(2,1)S(1)}, bf16[128,512]{1,0:T(8,128)(2,1)}, u32[]{:S(2)}) copy-start(bf16[128,512]{1,0:T(8,128)(2,1)} %param.7) | copy-start | bytes 393220
  128.5 16.5 %copy-start = (bf16[4,128,2048]{2,1,0:T(8,128)(2,1)S(1)}, bf16[4,128,2048]{2,1,0:T(8,128)(2,1)}, u32[]{:S(2)}) copy-start(bf16[4,128,2048]{2,1,0:T(8,128)(2,1)} %copy.26) | copy-start | bytes 6291460
  134.9 15.9 %copy-start.3 = (bf16[128,512]{1,0:T(8,128)(2,1)}, bf16[128,512]{1,0:T(8,128)(2,1)S(1)}, u32[]{:S(2)}) copy-start(bf16[128,512]{1,0:T(8,128)(2,1)S(1)} %subtract_convert_fusion) | copy-start | bytes 393220
Sparse Core Ops, SparseCore 0:
  13.5 99.2 all-reduce.1
Sparse Core Ops, SparseCore 1:
  55.1 24.6 reduce-scatter.1
where the time goes:
time: 163 us; the launch traced here: 162 us
  waiting for transfers between devices  44.5 us (27%)
  blocking collectives  40.5 us (25%)
  local copies, waits for them, and re-layouts  39.9 us (24%)
  between operations  15.5 us (10%)
  other arithmetic  11.3 us (7%)
  matrix products  10.4 us (6%)
    psum x1, waiting for transfers between devices, shards(): summed = lax.psum(pseudo[0], 'replica')  44.5 us
    unnamed x18, local copies, waits for them, and re-layouts  37.3 us
    all_to_all x1, blocking collectives, shards(): lax.all_to_all(tokens, 'fsdp', split_axis=1, concat_axis=0, tiled=True)  30.5 us
    add x1, other arithmetic, shards(): new_momentum = nesterov_coef * momentum + averaged  10.4 us
    all_gather x1, blocking collectives, shards(): residual_all = lax.all_gather(residual_own, 'fsdp', axis=0, tiled=True)  10 us
    dot_general x1, matrix products, shards(): lax.dot_general(columns, residual_all, (((0,), (0,)), ((), ())), preferre...  5.87 us
    dot_general x1, matrix products, shards(): jnp.dot(columns, weight_rows, preferred_element_type=jnp.float32)  4.49 us
  transfers between devices with their start and end apart: 2, of which 1 were waited for; matrix products, arithmetic and copies ran while one was open for 27% of the time, Pallas kernels for 0%

commit v1 on v0

v1 whole, which is shorter than its diff:
```python
import functools

import jax
import jax.numpy as jnp
from jax import lax
from jax.experimental import pallas as pl
from jax.experimental.pallas import tpu as pltpu
from jax.sharding import PartitionSpec as P

inner_rate = 1.0
outer_rate = 0.7
nesterov_coef = 0.9
merge_share = 0.5

MESH = pl.DeviceIdType.MESH
F32 = jnp.float32
BF16 = jnp.bfloat16


def partner(me, step, n):
    if n & (n - 1):
        return lax.rem(me + step, n)
    total, bit = 0, 1
    while bit < n:
        total = total + lax.rem(lax.div(me, bit) + (step // bit) % 2, 2) * bit
        bit *= 2
    return total


def exchange(
    nr, nf, nt, nc, scale,
    tok, tgt, wt, ps, gf, mom,
    xt, ra, ng, nm, res, wv,
    x, s, rv, tv, own, pair, sbuf, inbuf, tot, gfv, momv,
    load_sem, xl_sem, own_sem,
    xs_sem, xr_sem, ss_sem, sr_sem, rs_sem, rr_sem,
    ps_sem, pr_sem, is_sem, ir_sem, os_sem, or_sem, ts_sem, tr_sem,
):
    rep, me = lax.axis_index("replica"), lax.axis_index("fsdp")
    core, pos = lax.rem(rep, 2), lax.div(rep, 2)
    other = 1 - core
    length = nr // 2
    mid = length // 2
    low = pos < mid
    inward = (jnp.where(low, pos + 1, pos - 1) * 2 + core, me)
    outward = (jnp.where(low, jnp.maximum(pos - 1, 0), jnp.minimum(pos + 1, length - 1)) * 2 + core, me)
    twin = (pos * 2 + other, me)
    is_mid = (pos == mid - 1) | (pos == mid)
    kind = jnp.where(is_mid, 1, 0)
    has_up = (pos > 0) & (pos < length - 1)
    th, dblk = x.shape[2], x.shape[3]
    rc = own.shape[1]
    half = nc * rc
    peers = [partner(me, d, nf) for d in range(1, nf)]

    barrier = pltpu.get_barrier_semaphore()
    greet = [(rep, q) for q in peers] + [
        twin,
        (lax.rem(pos + 1, length) * 2 + core, me),
        (lax.rem(pos + length - 1, length) * 2 + core, me),
    ]
    for device in greet:
        pl.semaphore_signal(barrier, inc=1, device_id=device, device_id_type=MESH)

    def local(src, dst, sem):
        copy = pltpu.make_async_copy(src, dst, sem)
        copy.start()
        return copy

    def remote(src, dst, send, recv, device):
        return pltpu.make_async_remote_copy(
            src_ref=src, dst_ref=dst, send_sem=send, recv_sem=recv, device_id=device, device_id_type=MESH
        )

    def rows(which, c):
        return pl.ds(pl.multiple_of(which * half + c * rc, rc), rc)

    def block(h, q):
        return tok.at[pl.ds(h * th, th), pl.ds(pl.multiple_of(q * dblk, 128), dblk)]

    own_copies = [local(ps.at[0, rows(core, c)], own.at[c], own_sem.at[c]) for c in range(nc)]
    x_copies = [local(block(h, me), x.at[h, me], xl_sem.at[h]) for h in range(nt)]
    w_copy = local(wt.at[0], wv, load_sem.at[0])
    t_copy = local(tgt, tv, load_sem.at[1])

    pl.semaphore_wait(barrier, len(greet))

    def pair_copy(c):
        return remote(ps.at[0, rows(other, c)], pair.at[c], ps_sem.at[c], pr_sem.at[c], twin)

    def x_copy(h, i):
        return remote(block(h, peers[i]), x.at[h, me], xs_sem.at[h, i], xr_sem.at[h, me], (rep, peers[i]))

    def s_copy(h, i):
        return remote(s.at[h, peers[i]], rv.at[h, me], ss_sem.at[h, i], sr_sem.at[h, me], (rep, peers[i]))

    def r_copy(h, i):
        return remote(ra.at[h, me], ra.at[h, me], rs_sem.at[h, i], rr_sem.at[h, me], (rep, peers[i]))

    def in_copy(c):
        return remote(sbuf.at[c], inbuf.at[kind, c], is_sem.at[c], ir_sem.at[kind, c], inward)

    def out_copy(c):
        return remote(tot.at[core, c], tot.at[core, c], os_sem.at[c], or_sem.at[c], outward)

    def twin_copy(c):
        return remote(tot.at[core, c], tot.at[core, c], ts_sem.at[c], tr_sem.at[c], twin)

    def arrive(ref, sem):
        remote(ref, ref, sem, sem, twin).wait_recv()

    for c in range(nc):
        pair_copy(c).start()
    for h in range(nt):
        for i in range(nf - 1):
            x_copy(h, i).start()
    gf_copy = local(gf, gfv, load_sem.at[2])
    mom_copy = local(mom, momv, load_sem.at[3])

    def chip_sum(c):
        own_copies[c].wait()
        pair_copy(c).wait_recv()
        return own[c] + pair[c]

    def up_end(c):
        sbuf[c] = chip_sum(c).astype(BF16)
        in_copy(c).start()

    def up_inner(c):
        total = chip_sum(c)
        arrive(inbuf.at[0, c], ir_sem.at[0, c])
        sbuf[c] = (total + inbuf[0, c].astype(F32)).astype(BF16)
        in_copy(c).start()

    def outer_step(which, c):
        at = rows(which, c)
        averaged = tot[which, c].astype(F32) / nr
        moved = nesterov_coef * momv[at, :] + averaged
        nm[at, :] = moved
        ng[at, :] = gfv[at, :] - outer_rate * (averaged + nesterov_coef * moved)

    def down(c):
        @pl.when(is_mid)
        def _():
            arrive(inbuf.at[1, c], ir_sem.at[1, c])
            tot[core, c] = (sbuf[c].astype(F32) + inbuf[1, c].astype(F32)).astype(BF16)

        @pl.when(jnp.logical_not(is_mid))
        def _():
            arrive(tot.at[core, c], or_sem.at[c])

        @pl.when(has_up)
        def _():
            out_copy(c).start()

        twin_copy(c).start()
        outer_step(core, c)

    def down_twin(c):
        arrive(tot.at[other, c], tr_sem.at[c])
        outer_step(other, c)

    def keys(h):
        x_copies[h].wait()
        for q in peers:
            arrive(x.at[h, q], xr_sem.at[h, q])
        block_h = x[h].reshape(nf * th, dblk)
        part = jnp.dot(block_h, wv[...], preferred_element_type=F32) * scale
        s[h] = part.astype(BF16).reshape(nf, th, part.shape[1])
        for i in range(nf - 1):
            s_copy(h, i).start()
        rv[h, me] = s[h, me]
        xt[:, h * nf * th:(h + 1) * nf * th] = block_h.T

    def error(h):
        for q in peers:
            arrive(rv.at[h, q], sr_sem.at[h, q])
        at = pl.ds(h * th, th)
        total = rv[h, 0].astype(F32)
        for f in range(1, nf):
            total = total + rv[h, f].astype(F32)
        err = (total - tv[at, :].astype(F32)).astype(BF16)
        ra[h, me] = err
        for i in range(nf - 1):
            r_copy(h, i).start()
        res[at, :] = err

    @pl.when(jnp.logical_not(has_up))
    def _():
        for c in range(nc):
            up_end(c)

    w_copy.wait()
    t_copy.wait()

    per = max(nc // nt, 1)
    for k in range(nc + 2):
        if k < nc:
            pl.when(has_up)(functools.partial(up_inner, k))
        if k == 1:
            gf_copy.wait()
            mom_copy.wait()
        if 1 <= k <= nc:
            down(k - 1)
        if k >= 2:
            down_twin(k - 2)
        if k >= 1 and k % per == 0 and k // per <= nt:
            keys(k // per - 1)
        if k >= 2 and (k - 1) % per == 0 and 1 <= (k - 1) // per <= nt:
            error((k - 1) // per - 1)

    for h in range(nt):
        for q in peers:
            arrive(ra.at[h, q], rr_sem.at[h, q])
    for c in range(nc):
        pair_copy(c).wait_send()
        in_copy(c).wait_send()
        twin_copy(c).wait_send()

    @pl.when(has_up)
    def _():
        for c in range(nc):
            out_copy(c).wait_send()

    for h in range(nt):
        for i in range(nf - 1):
            x_copy(h, i).wait_send()
            s_copy(h, i).wait_send()
            r_copy(h, i).wait_send()


def merge(nb, scale, xt, ra, ng, nm, res, wv, nw_out, res_out, ng_out, nm_out, nw, sems, w_sems):
    copies = [
        pltpu.make_async_copy(nm, nm_out, sems.at[0]),
        pltpu.make_async_copy(ng, ng_out, sems.at[1]),
        pltpu.make_async_copy(res, res_out, sems.at[2]),
    ]
    for copy in copies:
        copy.start()
    width = xt.shape[0] // nb
    errors = ra[...].reshape(xt.shape[1], ra.shape[-1])
    for b in range(nb):
        at = pl.ds(b * width, width)
        gradient = jnp.dot(xt[at, :], errors, preferred_element_type=F32) * scale
        stepped = wv[at, :].astype(F32) - inner_rate * gradient
        nw[at, :] = (merge_share * stepped + (1.0 - merge_share) * ng[at, :]).astype(BF16)
        copy = pltpu.make_async_copy(nw.at[at], nw_out.at[0, at], w_sems.at[b])
        copy.start()
        copies.append(copy)
    for copy in copies:
        copy.wait()


def solution(mesh):
    nr, nf = mesh.shape["replica"], mesh.shape["fsdp"]

    def shards(tokens, target, weight, pseudo, global_frag, momentum):
        t, width = tokens.shape
        _, dblk, kv = weight.shape
        scale = width ** (-0.5)
        nt = 4
        nc = 8
        nb = 8
        th, rc = t // nt, dblk // 2 // nc
        any_ = pl.BlockSpec(memory_space=pltpu.HBM)
        vmem = pl.BlockSpec(memory_space=pltpu.VMEM)
        dma = pltpu.SemaphoreType.DMA
        middle = pl.pallas_call(
            functools.partial(exchange, nr, nf, nt, nc, scale),
            out_shape=(
                pltpu.VMEM((dblk, nt * nf * th), BF16),
                pltpu.VMEM((nt, nf, th, kv), BF16),
                pltpu.VMEM((dblk, kv), F32),
                pltpu.VMEM((dblk, kv), F32),
                pltpu.VMEM((t, kv), BF16),
                pltpu.VMEM((dblk, kv), BF16),
            ),
            in_specs=[any_] * 6,
            out_specs=(vmem,) * 6,
            scratch_shapes=[
                pltpu.VMEM((nt, nf, th, dblk), BF16),
                pltpu.VMEM((nt, nf, th, kv), BF16),
                pltpu.VMEM((nt, nf, th, kv), BF16),
                pltpu.VMEM((t, kv), BF16),
                pltpu.VMEM((nc, rc, kv), F32),
                pltpu.VMEM((nc, rc, kv), F32),
                pltpu.VMEM((nc, rc, kv), BF16),
                pltpu.VMEM((2, nc, rc, kv), BF16),
                pltpu.VMEM((2, nc, rc, kv), BF16),
                pltpu.VMEM((dblk, kv), F32),
                pltpu.VMEM((dblk, kv), F32),
                dma((4,)), dma((nt,)), dma((nc,)),
                dma((nt, nf)), dma((nt, nf)), dma((nt, nf)), dma((nt, nf)), dma((nt, nf)), dma((nt, nf)),
                dma((nc,)), dma((nc,)), dma((nc,)), dma((2, nc)), dma((nc,)), dma((nc,)), dma((nc,)), dma((nc,)),
            ],
            compiler_params=pltpu.CompilerParams(
                collective_id=0, has_side_effects=True, vmem_limit_bytes=40 << 20
            ),
            name="exchange",
        )(tokens, target, weight, pseudo, global_frag, momentum)
        return pl.pallas_call(
            functools.partial(merge, nb, scale),
            out_shape=(
                jax.ShapeDtypeStruct((1, dblk, kv), BF16),
                jax.ShapeDtypeStruct((t, kv), BF16),
                jax.ShapeDtypeStruct((dblk, kv), F32),
                jax.ShapeDtypeStruct((dblk, kv), F32),
            ),
            in_specs=[vmem] * 6,
            out_specs=(any_,) * 4,
            scratch_shapes=[pltpu.VMEM((dblk, kv), BF16), dma((3,)), dma((nb,))],
            compiler_params=pltpu.CompilerParams(vmem_limit_bytes=40 << 20),
            name="merge",
        )(*middle)

    in_specs = (
        P(("replica", "fsdp"), None),
        P(("replica", "fsdp"), None),
        P("replica", "fsdp", None),
        P("replica", "fsdp", None),
        P("fsdp", None),
        P("fsdp", None),
    )
    out_specs = (
        P("replica", "fsdp", None),
        P(("replica", "fsdp"), None),
        P("fsdp", None),
        P("fsdp", None),
    )
    return jax.shard_map(shards, mesh=mesh, in_specs=in_specs, out_specs=out_specs, check_vma=False)
```

time: 163 us -> 64.9 us (0.40)
  Pallas kernels: 0 us -> 63.2 us
  waiting for transfers between devices: 44.5 us -> 0 us
  blocking collectives: 40.5 us -> 0 us
  local copies, waits for them, and re-layouts: 39.9 us -> 0.9 us
  between operations: 15.5 us -> 0.65 us
  other arithmetic: 11.3 us -> 0 us
  matrix products: 10.4 us -> 0 us
    pallas_call x0 -> x2, Pallas kernels: none -> 63.2 us  [the longest x1 58.2 us: shards(): pl.pallas_call(functools.partial(exchange, nr, nf, nt, nc, scale), out_sh...]
    psum x1 -> x0, waiting for transfers between devices: 44.5 us -> none  [shards(): summed = lax.psum(pseudo[0], 'replica')]
    unnamed x18 -> x2, local copies, waits for them, and re-layouts: 37.3 us -> 0.9 us
    all_to_all x1 -> x0, blocking collectives: 30.5 us -> none  [shards(): lax.all_to_all(tokens, 'fsdp', split_axis=1, concat_axis=0, tiled=True)]
    dot_general x2 -> x0, matrix products: 10.4 us -> none  [the longest x1 5.87 us: shards(): lax.dot_general(columns, residual_all, (((0,), (0,)), ((), ())), preferre...]
    add x1 -> x0, other arithmetic: 10.4 us -> none  [shards(): new_momentum = nesterov_coef * momentum + averaged]
    all_gather x1 -> x0, blocking collectives: 10 us -> none  [shards(): residual_all = lax.all_gather(residual_own, 'fsdp', axis=0, tiled=True)]
    all_to_all x1 -> x0, local copies, waits for them, and re-layouts: 2.58 us -> none  [shards(): lax.all_to_all(tokens, 'fsdp', split_axis=1, concat_axis=0, tiled=True)]
  transfers between devices with their start and end apart: 2 -> 0, of which waited for: 1 -> 0; matrix products, arithmetic and copies ran while one was open for 27% -> 0% of each run, Pallas kernels for 0% -> 0%
where the time goes in v1:
time: 64.9 us; the launch traced here: 64.7 us
  Pallas kernels  63.2 us (97%)
  local copies, waits for them, and re-layouts  0.9 us (1%)
  between operations  0.65 us (1%)
    pallas_call x1, Pallas kernels, shards(): pl.pallas_call(functools.partial(exchange, nr, nf, nt, nc, scale), out_sh...  58.2 us
    pallas_call x1, Pallas kernels, shards(): pl.pallas_call(functools.partial(merge, nb, scale), out_shape=(jax.ShapeD...  4.93 us

profile of v1, /device:TPU:0, one launch (start us, length us, event | category | flops | bytes accessed | tf_op | source)
XLA Modules:
  0.0 64.7 jit_solution(2519151952653966288)
XLA Ops:
  0.6 0.0 copy-start
  0.6 0.9 %copy-done = bf16[128,512]{1,0:T(8,128)(2,1)S(1)} copy-done((bf16[128,512]{1,0:T(8,128)(2,1)S(1)}, bf16[128,512]{1,0:T(8,128)(2,1)}, u32[]{:S(2)}) %copy-start) | copy-done | bytes 131096
  1.5 58.2 %exchange.1 = (bf16[2048,512]{1,0:T(8,128)(2,1)S(1)}, bf16[4,4,32,512]{3,2,1,0:T(8,128)(2,1)S(1)}, f32[2048,512]{1,0:T(8,128)S(1)}, f32[2048,512]{1,0:T(8,128)S(...) custom-call(bf16[128,8192]{1,0:T(8,128)(2,1)} %tok.1, bf16[128,512]{1,0:T(8,128)(2,1)S(1)} %copy-done, ...), custom_call_target="tpu_custom_call" | custom-call | tf_op jit(solution)/shard_map/exchange/pallas_call | solution.py:268
  59.8 4.9 %merge.1 = (bf16[1,2048,512]{2,1,0:T(8,128)(2,1)}, bf16[128,512]{1,0:T(8,128)(2,1)}, f32[2048,512]{1,0:T(8,128)}, f32[2048,512]{1,0:T(8,128)}) custom-call(bf16[2048,512]{1,0:T(8,128)(2,1)S(1)} %get-tuple-element.10.xt, bf16[4,4,32,512]{3,2,1,0:T(8,128)(2,1)S(1)} %get-tuple-element.11.ra, f32[2048,512]{1,0:T(8,128)S(1)} %get-tuple-element.12.ng, ...), custom_call_target="tpu_custom_call" | custom-call | tf_op jit(solution)/shard_map/merge/pallas_call | solution.py:301
Async XLA Ops:
  0.6 0.9 %copy-start = (bf16[128,512]{1,0:T(8,128)(2,1)S(1)}, bf16[128,512]{1,0:T(8,128)(2,1)}, u32[]{:S(2)}) copy-start(bf16[128,512]{1,0:T(8,128)(2,1)} %tgt.1) | copy-start | bytes 393220

commit v2 on v1

--- a/solution.py
+++ b/solution.py
@@ -51,7 +51,7 @@
     th, dblk = x.shape[2], x.shape[3]
     rc = own.shape[1]
     half = nc * rc
-    peers = [partner(me, d, nf) for d in range(1, nf)]
+    peers = [partner(me, d, nf) for d in range(nf - 1, 0, -1)]
 
     barrier = pltpu.get_barrier_semaphore()
     greet = [(rep, q) for q in peers] + [
@@ -193,7 +193,7 @@
     w_copy.wait()
     t_copy.wait()
 
-    per = max(nc // nt, 1)
+    key_at, error_at = (3, 6), (5, 8)
     for k in range(nc + 2):
         if k < nc:
             pl.when(has_up)(functools.partial(up_inner, k))
@@ -204,10 +204,11 @@
             down(k - 1)
         if k >= 2:
             down_twin(k - 2)
-        if k >= 1 and k % per == 0 and k // per <= nt:
-            keys(k // per - 1)
-        if k >= 2 and (k - 1) % per == 0 and 1 <= (k - 1) // per <= nt:
-            error((k - 1) // per - 1)
+        for h in range(nt):
+            if k == key_at[h]:
+                keys(h)
+            if k == error_at[h]:
+                error(h)
 
     for h in range(nt):
         for q in peers:
@@ -229,15 +230,19 @@
             r_copy(h, i).wait_send()
 
 
-def merge(nb, scale, xt, ra, ng, nm, res, wv, nw_out, res_out, ng_out, nm_out, nw, sems, w_sems):
+def merge(nb, scale, xt, ra, ng, nm, res, wv, nw_out, res_out, ng_out, nm_out, nw, sems, w_sems, o_sems):
     copies = [
-        pltpu.make_async_copy(nm, nm_out, sems.at[0]),
-        pltpu.make_async_copy(ng, ng_out, sems.at[1]),
         pltpu.make_async_copy(res, res_out, sems.at[2]),
     ]
     for copy in copies:
         copy.start()
     width = xt.shape[0] // nb
+    for b in range(nb):
+        at = pl.ds(b * width, width)
+        for i, (src, dst) in enumerate(((nm, nm_out), (ng, ng_out))):
+            copy = pltpu.make_async_copy(src.at[at], dst.at[at], o_sems.at[i, b])
+            copy.start()
+            copies.append(copy)
     errors = ra[...].reshape(xt.shape[1], ra.shape[-1])
     for b in range(nb):
         at = pl.ds(b * width, width)
@@ -258,7 +263,7 @@
         t, width = tokens.shape
         _, dblk, kv = weight.shape
         scale = width ** (-0.5)
-        nt = 4
+        nt = 2
         nc = 8
         nb = 8
         th, rc = t // nt, dblk // 2 // nc
@@ -308,7 +313,7 @@
             ),
             in_specs=[vmem] * 6,
             out_specs=(any_,) * 4,
-            scratch_shapes=[pltpu.VMEM((dblk, kv), BF16), dma((3,)), dma((nb,))],
+            scratch_shapes=[pltpu.VMEM((dblk, kv), BF16), dma((3,)), dma((nb,)), dma((2, nb))],
             compiler_params=pltpu.CompilerParams(vmem_limit_bytes=40 << 20),
             name="merge",
         )(*middle)

time: 64.9 us -> 56.1 us (0.86)
  Pallas kernels: 63.2 us -> 54.4 us
    pallas_call x1, Pallas kernels: 58.2 us -> 49.7 us  [shards(): pl.pallas_call(functools.partial(exchange, nr, nf, nt, nc, scale), out_sh...]
where the time goes in v2:
time: 56.1 us; the launch traced here: 56 us
  Pallas kernels  54.4 us (97%)
  local copies, waits for them, and re-layouts  0.9 us (2%)
  between operations  0.65 us (1%)
    pallas_call x1, Pallas kernels, shards(): pl.pallas_call(functools.partial(exchange, nr, nf, nt, nc, scale), out_sh...  49.7 us
    pallas_call x1, Pallas kernels, shards(): pl.pallas_call(functools.partial(merge, nb, scale), out_shape=(jax.ShapeD...  4.7 us

profile of v2, /device:TPU:0, one launch (start us, length us, event | category | flops | bytes accessed | tf_op | source)
XLA Modules:
  0.0 56.0 jit_solution(3842610136339090854)
XLA Ops:
  0.6 0.0 copy-start
  0.6 0.9 %copy-done = bf16[128,512]{1,0:T(8,128)(2,1)S(1)} copy-done((bf16[128,512]{1,0:T(8,128)(2,1)S(1)}, bf16[128,512]{1,0:T(8,128)(2,1)}, u32[]{:S(2)}) %copy-start) | copy-done | bytes 131096
  1.5 49.7 %exchange.1 = (bf16[2048,512]{1,0:T(8,128)(2,1)S(1)}, bf16[2,4,64,512]{3,2,1,0:T(8,128)(2,1)S(1)}, f32[2048,512]{1,0:T(8,128)S(1)}, f32[2048,512]{1,0:T(8,128)S(...) custom-call(bf16[128,8192]{1,0:T(8,128)(2,1)} %tok.1, bf16[128,512]{1,0:T(8,128)(2,1)S(1)} %copy-done, ...), custom_call_target="tpu_custom_call" | custom-call | tf_op jit(solution)/shard_map/exchange/pallas_call | solution.py:273
  51.3 4.7 %merge.1 = (bf16[1,2048,512]{2,1,0:T(8,128)(2,1)}, bf16[128,512]{1,0:T(8,128)(2,1)}, f32[2048,512]{1,0:T(8,128)}, f32[2048,512]{1,0:T(8,128)}) custom-call(bf16[2048,512]{1,0:T(8,128)(2,1)S(1)} %get-tuple-element.10.xt, bf16[2,4,64,512]{3,2,1,0:T(8,128)(2,1)S(1)} %get-tuple-element.11.ra, f32[2048,512]{1,0:T(8,128)S(1)} %get-tuple-element.12.ng, ...), custom_call_target="tpu_custom_call" | custom-call | tf_op jit(solution)/shard_map/merge/pallas_call | solution.py:306
Async XLA Ops:
  0.6 0.9 %copy-start = (bf16[128,512]{1,0:T(8,128)(2,1)S(1)}, bf16[128,512]{1,0:T(8,128)(2,1)}, u32[]{:S(2)}) copy-start(bf16[128,512]{1,0:T(8,128)(2,1)} %tgt.1) | copy-start | bytes 393220

commit v3 on v2

--- a/solution.py
+++ b/solution.py
@@ -28,7 +28,7 @@
 
 
 def exchange(
-    nr, nf, nt, nc, scale,
+    nr, nf, parts, nc, scale,
     tok, tgt, wt, ps, gf, mom,
     xt, ra, ng, nm, res, wv,
     x, s, rv, tv, own, pair, sbuf, inbuf, tot, gfv, momv,
@@ -37,6 +37,7 @@
     ps_sem, pr_sem, is_sem, ir_sem, os_sem, or_sem, ts_sem, tr_sem,
 ):
     rep, me = lax.axis_index("replica"), lax.axis_index("fsdp")
+    nt = len(parts)
     core, pos = lax.rem(rep, 2), lax.div(rep, 2)
     other = 1 - core
     length = nr // 2
@@ -48,7 +49,7 @@
     is_mid = (pos == mid - 1) | (pos == mid)
     kind = jnp.where(is_mid, 1, 0)
     has_up = (pos > 0) & (pos < length - 1)
-    th, dblk = x.shape[2], x.shape[3]
+    dblk = x.shape[1]
     rc = own.shape[1]
     half = nc * rc
     peers = [partner(me, d, nf) for d in range(nf - 1, 0, -1)]
@@ -75,11 +76,22 @@
     def rows(which, c):
         return pl.ds(pl.multiple_of(which * half + c * rc, rc), rc)
 
+    first = [sum(parts[:h]) for h in range(nt)]
+
+    def own_rows(h):
+        return pl.ds(first[h], parts[h])
+
+    def at_rows(h, q):
+        return pl.ds(pl.multiple_of(nf * first[h] + q * parts[h], 16), parts[h])
+
+    def all_rows(h):
+        return pl.ds(nf * first[h], nf * parts[h])
+
     def block(h, q):
-        return tok.at[pl.ds(h * th, th), pl.ds(pl.multiple_of(q * dblk, 128), dblk)]
+        return tok.at[own_rows(h), pl.ds(pl.multiple_of(q * dblk, 128), dblk)]
 
     own_copies = [local(ps.at[0, rows(core, c)], own.at[c], own_sem.at[c]) for c in range(nc)]
-    x_copies = [local(block(h, me), x.at[h, me], xl_sem.at[h]) for h in range(nt)]
+    x_copies = [local(block(h, me), x.at[at_rows(h, me)], xl_sem.at[h]) for h in range(nt)]
     w_copy = local(wt.at[0], wv, load_sem.at[0])
     t_copy = local(tgt, tv, load_sem.at[1])
 
@@ -89,13 +101,13 @@
         return remote(ps.at[0, rows(other, c)], pair.at[c], ps_sem.at[c], pr_sem.at[c], twin)
 
     def x_copy(h, i):
-        return remote(block(h, peers[i]), x.at[h, me], xs_sem.at[h, i], xr_sem.at[h, me], (rep, peers[i]))
+        return remote(block(h, peers[i]), x.at[at_rows(h, me)], xs_sem.at[h, i], xr_sem.at[h, me], (rep, peers[i]))
 
     def s_copy(h, i):
-        return remote(s.at[h, peers[i]], rv.at[h, me], ss_sem.at[h, i], sr_sem.at[h, me], (rep, peers[i]))
+        return remote(s.at[at_rows(h, peers[i])], rv.at[at_rows(h, me)], ss_sem.at[h, i], sr_sem.at[h, me], (rep, peers[i]))
 
     def r_copy(h, i):
-        return remote(ra.at[h, me], ra.at[h, me], rs_sem.at[h, i], rr_sem.at[h, me], (rep, peers[i]))
+        return remote(ra.at[at_rows(h, me)], ra.at[at_rows(h, me)], rs_sem.at[h, i], rr_sem.at[h, me], (rep, peers[i]))
 
     def in_copy(c):
         return remote(sbuf.at[c], inbuf.at[kind, c], is_sem.at[c], ir_sem.at[kind, c], inward)
@@ -163,24 +175,24 @@
     def keys(h):
         x_copies[h].wait()
         for q in peers:
-            arrive(x.at[h, q], xr_sem.at[h, q])
-        block_h = x[h].reshape(nf * th, dblk)
+            arrive(x.at[at_rows(h, q)], xr_sem.at[h, q])
+        block_h = x[all_rows(h), :]
         part = jnp.dot(block_h, wv[...], preferred_element_type=F32) * scale
-        s[h] = part.astype(BF16).reshape(nf, th, part.shape[1])
+        s[all_rows(h), :] = part.astype(BF16)
         for i in range(nf - 1):
             s_copy(h, i).start()
-        rv[h, me] = s[h, me]
-        xt[:, h * nf * th:(h + 1) * nf * th] = block_h.T
+        rv[at_rows(h, me), :] = s[at_rows(h, me), :]
+        xt[:, all_rows(h)] = block_h.T
 
     def error(h):
         for q in peers:
-            arrive(rv.at[h, q], sr_sem.at[h, q])
-        at = pl.ds(h * th, th)
-        total = rv[h, 0].astype(F32)
+            arrive(rv.at[at_rows(h, q)], sr_sem.at[h, q])
+        at = own_rows(h)
+        total = rv[at_rows(h, 0), :].astype(F32)
         for f in range(1, nf):
-            total = total + rv[h, f].astype(F32)
+            total = total + rv[at_rows(h, f), :].astype(F32)
         err = (total - tv[at, :].astype(F32)).astype(BF16)
-        ra[h, me] = err
+        ra[at_rows(h, me), :] = err
         for i in range(nf - 1):
             r_copy(h, i).start()
         res[at, :] = err
@@ -193,7 +205,7 @@
     w_copy.wait()
     t_copy.wait()
 
-    key_at, error_at = (3, 6), (5, 8)
+    key_at, error_at = (5, 6), (7, 8)
     for k in range(nc + 2):
         if k < nc:
             pl.when(has_up)(functools.partial(up_inner, k))
@@ -212,7 +224,7 @@
 
     for h in range(nt):
         for q in peers:
-            arrive(ra.at[h, q], rr_sem.at[h, q])
+            arrive(ra.at[at_rows(h, q)], rr_sem.at[h, q])
     for c in range(nc):
         pair_copy(c).wait_send()
         in_copy(c).wait_send()
@@ -243,7 +255,7 @@
             copy = pltpu.make_async_copy(src.at[at], dst.at[at], o_sems.at[i, b])
             copy.start()
             copies.append(copy)
-    errors = ra[...].reshape(xt.shape[1], ra.shape[-1])
+    errors = ra[...]
     for b in range(nb):
         at = pl.ds(b * width, width)
         gradient = jnp.dot(xt[at, :], errors, preferred_element_type=F32) * scale
@@ -263,18 +275,19 @@
         t, width = tokens.shape
         _, dblk, kv = weight.shape
         scale = width ** (-0.5)
-        nt = 2
+        parts = (t * 3 // 4, t - t * 3 // 4)
+        nt = len(parts)
         nc = 8
         nb = 8
-        th, rc = t // nt, dblk // 2 // nc
+        rc = dblk // 2 // nc
         any_ = pl.BlockSpec(memory_space=pltpu.HBM)
         vmem = pl.BlockSpec(memory_space=pltpu.VMEM)
         dma = pltpu.SemaphoreType.DMA
         middle = pl.pallas_call(
-            functools.partial(exchange, nr, nf, nt, nc, scale),
+            functools.partial(exchange, nr, nf, parts, nc, scale),
             out_shape=(
-                pltpu.VMEM((dblk, nt * nf * th), BF16),
-                pltpu.VMEM((nt, nf, th, kv), BF16),
+                pltpu.VMEM((dblk, nf * t), BF16),
+                pltpu.VMEM((nf * t, kv), BF16),
                 pltpu.VMEM((dblk, kv), F32),
                 pltpu.VMEM((dblk, kv), F32),
                 pltpu.VMEM((t, kv), BF16),
@@ -283,9 +296,9 @@
             in_specs=[any_] * 6,
             out_specs=(vmem,) * 6,
             scratch_shapes=[
-                pltpu.VMEM((nt, nf, th, dblk), BF16),
-                pltpu.VMEM((nt, nf, th, kv), BF16),
-                pltpu.VMEM((nt, nf, th, kv), BF16),
+                pltpu.VMEM((nf * t, dblk), BF16),
+                pltpu.VMEM((nf * t, kv), BF16),
+                pltpu.VMEM((nf * t, kv), BF16),
                 pltpu.VMEM((t, kv), BF16),
                 pltpu.VMEM((nc, rc, kv), F32),
                 pltpu.VMEM((nc, rc, kv), F32),

time: 56.1 us -> 54.1 us (0.964)
  Pallas kernels: 54.4 us -> 52.4 us
    pallas_call x1, Pallas kernels: 49.7 us -> 47.7 us  [shards(): pl.pallas_call(functools.partial(exchange, nr, nf, parts, nc, scale), out...]
where the time goes in v3:
time: 54.1 us; the launch traced here: 53.9 us
  Pallas kernels  52.4 us (97%)
  local copies, waits for them, and re-layouts  0.9 us (2%)
  between operations  0.65 us (1%)
    pallas_call x1, Pallas kernels, shards(): pl.pallas_call(functools.partial(exchange, nr, nf, parts, nc, scale), out...  47.7 us
    pallas_call x1, Pallas kernels, shards(): pl.pallas_call(functools.partial(merge, nb, scale), out_shape=(jax.ShapeD...  4.7 us

profile of v3, /device:TPU:0, one launch (start us, length us, event | category | flops | bytes accessed | tf_op | source)
XLA Modules:
  0.0 53.9 jit_solution(1918053838593307396)
XLA Ops:
  0.6 0.0 copy-start
  0.6 0.9 %copy-done = bf16[128,512]{1,0:T(8,128)(2,1)S(1)} copy-done((bf16[128,512]{1,0:T(8,128)(2,1)S(1)}, bf16[128,512]{1,0:T(8,128)(2,1)}, u32[]{:S(2)}) %copy-start) | copy-done | bytes 131096
  1.5 47.7 %exchange.1 = (bf16[2048,512]{1,0:T(8,128)(2,1)S(1)}, bf16[512,512]{1,0:T(8,128)(2,1)S(1)}, f32[2048,512]{1,0:T(8,128)S(1)}, f32[2048,512]{1,0:T(8,128)S(1)}, bf...) custom-call(bf16[128,8192]{1,0:T(8,128)(2,1)} %tok.1, bf16[128,512]{1,0:T(8,128)(2,1)S(1)} %copy-done, ...), custom_call_target="tpu_custom_call" | custom-call | tf_op jit(solution)/shard_map/exchange/pallas_call | solution.py:286
  49.2 4.7 %merge.1 = (bf16[1,2048,512]{2,1,0:T(8,128)(2,1)}, bf16[128,512]{1,0:T(8,128)(2,1)}, f32[2048,512]{1,0:T(8,128)}, f32[2048,512]{1,0:T(8,128)}) custom-call(bf16[2048,512]{1,0:T(8,128)(2,1)S(1)} %get-tuple-element.10.xt, bf16[512,512]{1,0:T(8,128)(2,1)S(1)} %get-tuple-element.11.ra, f32[2048,512]{1,0:T(8,128)S(1)} %get-tuple-element.12.ng, ...), custom_call_target="tpu_custom_call" | custom-call | tf_op jit(solution)/shard_map/merge/pallas_call | solution.py:319
Async XLA Ops:
  0.6 0.9 %copy-start = (bf16[128,512]{1,0:T(8,128)(2,1)S(1)}, bf16[128,512]{1,0:T(8,128)(2,1)}, u32[]{:S(2)}) copy-start(bf16[128,512]{1,0:T(8,128)(2,1)} %tgt.1) | copy-start | bytes 393220
